TPU v7x, 32 devices: a whole 2x2x4 slice. The times are simulated.
32 devices in a mesh: row: 4 (over y, core), col: 8 (over z, x).
Axes of the slice: x: 2, y: 2, z: 4, core: 2. Of those that a mesh axis runs over, the one named last changes fastest.
Arguments:
- features: bfloat16 [8192, 256], P(('col', 'row')), may hold values from -6 to 6
- adj_tiles: bfloat16 [4, 8, 16, 256, 256], P('row', 'col'), may hold values from -0.1875 to 0.1875
- tile_rows: int32 [4, 8, 16], P('row', 'col'), may hold values from 0 to 7, as said below
- tile_cols: int32 [4, 8, 16], P('row', 'col'), may hold values from 0 to 3, as said below
- tile_count: int32 [4, 8], P('row', 'col'), may hold values from 1 to 16, as said below
- weight: bfloat16 [256, 256], replicated, may hold values from -0.375 to 0.375
- grad_out: bfloat16 [8192, 256], P(('row', 'col')), may hold values from -6 to 6
Outputs:
- activation: bfloat16 [8192, 256], P(('row', 'col'))
- weight_grad: float32 [256, 256], replicated
- x_grad: bfloat16 [8192, 256], P(('col', 'row'))
Inputs may be any that keep to these rules, and one draw needn't show every extreme that they name: On each grid block the 16 slots name distinct tile positions (tile_rows, tile_cols). `tile_cols`: paired with tile_rows slot by slot. `tile_count`: slots of a grid block at or beyond its count are ignored.
All inputs are finite; a program needn't handle non-finite values.
Results may differ from a plain program's by a relative error of at most 0.025.
Values may be sent and summed in bfloat16 or wider, within the bound.
A program may use at most 128 MiB of HBM per device.

v0:
```python
import functools
import math

import jax
import jax.numpy as jnp
from jax import lax
from jax.experimental import pallas as pl
from jax.experimental.pallas import tpu as pltpu
from jax.sharding import PartitionSpec as P

MESH = pl.DeviceIdType.MESH
BF16 = jnp.bfloat16
F32 = jnp.float32
Q = 2


def dot(a, b):
    return jnp.dot(a, b, preferred_element_type=F32)


def kernel(
    R, C, S, T, F, scale,
    feat, adj, trow, tcol, tcnt, wt, gout,
    act_out, wg_out, xg_out,
    tiles, xs, wv, gv, rows_s, cols_s, cnt_s, pos, inv, accf,
    xsend, xrecv, zsend, zrecv, actv, mt, bacc,
    bsend, brecv, osend, orecv, xgv,
    wterm, wr1, wr2, wr3, wgv,
    loc, fs, fr, ps, pr, zs, zr, ms, mr, bs, br, os_, or_,
    w1s, w1r, w2s, w2r, w3s, w3r,
):
    r = lax.axis_index("row")
    c = lax.axis_index("col")
    Ro, Z = R // 2, C // 2
    yo, k = r // 2, r % 2
    z, x = c // 2, c % 2
    inner = yo * 2 + 1 - k
    xpeer = z * 2 + 1 - x
    H = T // C

    def remote(src, dst, ss, rs, row, col):
        return pltpu.make_async_remote_copy(
            src_ref=src, dst_ref=dst, send_sem=ss, recv_sem=rs,
            device_id={"row": row, "col": col}, device_id_type=MESH,
        )

    def arrived(dst, rs):
        pltpu.make_async_copy(dst, dst, rs).wait()

    c_feat = pltpu.make_async_copy(feat, xs.at[r], loc.at[0])
    c_feat.start()
    c_adj = pltpu.make_async_copy(adj.at[0, 0], tiles.at[pl.ds(0, S)], loc.at[1])
    c_adj.start()
    c_w = pltpu.make_async_copy(wt, wv, loc.at[2])
    c_w.start()
    c_g = pltpu.make_async_copy(gout, gv, loc.at[3])
    c_g.start()

    c_ids = [
        pltpu.make_async_copy(src, dst, loc.at[7 + n])
        for n, (src, dst) in enumerate(((trow, rows_s), (tcol, cols_s), (tcnt, cnt_s)))
    ]
    for cp in c_ids:
        cp.start()

    barrier = pltpu.get_barrier_semaphore()
    for o in range(1, R):
        pl.semaphore_signal(
            barrier, inc=1, device_id={"row": (r + o) % R, "col": c}, device_id_type=MESH)
    for o in range(1, C):
        pl.semaphore_signal(
            barrier, inc=1, device_id={"row": r, "col": (c + o) % C}, device_id_type=MESH)
    pl.semaphore_wait(barrier, R - 1 + C - 1)

    c_feat.wait()
    fcopies = []
    for o in range(1, Ro):
        cp = remote(xs.at[r], xs.at[r], fs.at[o], fr.at[r], ((yo + o) % Ro) * 2 + k, c)
        cp.start()
        fcopies.append(cp)
    cp = remote(xs.at[r], xs.at[r], fs.at[0], fr.at[r], inner, c)
    cp.start()
    fcopies.append(cp)

    tiles[S] = jnp.zeros((T, T), BF16)
    for cp in c_ids:
        cp.wait()
    total = cnt_s[0, 0]

    def set_pos(s, _):
        pos[s] = jnp.where(s < total, rows_s[0, 0, s] * R + cols_s[0, 0, s], -1)
        return 0

    lax.fori_loop(0, S, set_pos, 0)

    def set_inv(p, _):
        slot = jnp.int32(S)
        for s in range(S):
            slot = jnp.where(pos[s] == p, jnp.int32(s), slot)
        inv[p] = slot
        return 0

    lax.fori_loop(0, C * R, set_inv, 0)

    for o in range(1, Ro):
        j = ((yo - o + Ro) % Ro) * 2 + k
        arrived(xs.at[j], fr.at[j])
        cp = remote(xs.at[j], xs.at[j], fs.at[Ro - 1 + o], fr.at[j], inner, c)
        cp.start()
        fcopies.append(cp)
    arrived(xs.at[inner], fr.at[inner])
    c_adj.wait()
    for o in range(1, Ro):
        j = ((yo - o + Ro) % Ro) * 2 + 1 - k
        arrived(xs.at[j], fr.at[j])

    tables = [sorted(range(Z), key=lambda d, zz=zz: (-abs(d - zz), d)) for zz in range(Z)]
    order = []
    for kk in range(Z):
        v = jnp.int32(tables[0][kk])
        for zz in range(1, Z):
            v = jnp.where(z == zz, jnp.int32(tables[zz][kk]), v)
        order.append(v)

    def pick(n):
        v = order[0]
        for kk in range(1, Z):
            v = jnp.where(n == kk, order[kk], v)
        return v

    def partial(i):
        total = dot(tiles[inv[i * R]], xs[0])
        for j in range(1, R):
            total += dot(tiles[inv[i * R + j]], xs[j])
        return total

    def px(n, q):
        return remote(xsend.at[n, q], xrecv.at[n, q], ps.at[n, q], pr.at[n, q], r, xpeer)

    def fwd_peer(n, _):
        xsend[n] = partial(pick(n) * 2 + 1 - x).astype(BF16).reshape(Q, T // Q, F)
        for q in range(Q):
            px(n, q).start()
        return 0

    lax.fori_loop(0, Z, fwd_peer, 0)

    def pz(n, d, q):
        right = d > z
        way = jnp.where(right, 0, 1)
        nxt = jnp.where(right, z + 1, z - 1)
        return remote(zsend.at[n, q], zrecv.at[way, d, q], zs.at[n, q], zr.at[way, d, q], r,
                      nxt * 2 + x)

    def fwd_chain(n, _):
        d = pick(n)
        accf[...] = partial(d * 2 + x).reshape(Q, T // Q, F)

        def piece(q, _):
            arrived(xrecv.at[n, q], pr.at[n, q])
            accf[q] += xrecv[n, q].astype(F32)

            @pl.when((d >= z) & (z > 0))
            def _():
                arrived(zrecv.at[0, d, q], zr.at[0, d, q])
                accf[q] += zrecv[0, d, q].astype(F32)

            @pl.when((d <= z) & (z < Z - 1))
            def _():
                arrived(zrecv.at[1, d, q], zr.at[1, d, q])
                accf[q] += zrecv[1, d, q].astype(F32)

            @pl.when(d != z)
            def _():
                zsend[n, q] = accf[q].astype(BF16)
                pz(n, d, q).start()

            return 0

        lax.fori_loop(0, Q, piece, 0)
        return 0

    lax.fori_loop(0, Z, fwd_chain, 0)

    c_w.wait()
    c_g.wait()
    agg = accf[...].reshape(T, F).astype(BF16)
    pre = dot(agg, wv[...])
    sig = jax.nn.sigmoid(pre)
    grad = (gv[...].astype(F32) * sig * (1.0 + pre * (1.0 - sig))).astype(BF16)
    mt[c] = lax.dot_general(
        wv[...], grad, (((1,), (1,)), ((), ())), preferred_element_type=F32
    ).astype(BF16).reshape(Q, F // Q, T)

    def to_z(n, s, q, way):
        i = s * 2 + x
        return remote(mt.at[i, q], mt.at[i, q], ms.at[way, n, q], mr.at[i, q], r,
                      (z + 1 - 2 * way) * 2 + x)

    def to_peer(n, s, q):
        i = s * 2 + x
        return remote(mt.at[i, q], mt.at[i, q], ms.at[2, n, q], mr.at[i, q], r, xpeer)

    def spread(n, s, q, act):
        @pl.when((s <= z) & (z < Z - 1))
        def _():
            act(to_z(n, s, q, 0))

        @pl.when((s >= z) & (z > 0))
        def _():
            act(to_z(n, s, q, 1))

        act(to_peer(n, s, q))

    for q in range(Q):
        spread(0, z, q, lambda cp: cp.start())

    actv[...] = (pre * sig).astype(BF16)
    c_act = pltpu.make_async_copy(actv, act_out, loc.at[4])
    c_act.start()

    aggt = jnp.transpose(agg.astype(F32)).astype(BF16)
    wterm[...] = dot(aggt, grad).astype(BF16)
    w1copies = []
    for o in range(1, C):
        to = (c + o) % C
        cp = remote(wterm.at[pl.ds(pl.multiple_of(to * H, H), H)], wr1.at[o], w1s.at[o],
                    w1r.at[o], r, to)
        cp.start()
        w1copies.append(cp)

    for j in range(R):
        bacc[j] = jnp.zeros((F, T), F32)

    def bwd_step(n):
        @pl.when((n > 0) & (n < Z))
        def _():
            s = pick(Z - 1 - n)
            i = s * 2 + x
            for q in range(Q):
                arrived(mt.at[i, q], mr.at[i, q])
                spread(n, s, q, lambda cp: cp.start())

        def half(h, _):
            m = n - h

            @pl.when((m >= 0) & (m < Z))
            def _():
                s = pick(Z - 1 - m)
                i = s * 2 + jnp.where(h == 0, x, 1 - x)

                @pl.when(h == 1)
                def _():
                    for q in range(Q):
                        arrived(mt.at[i, q], mr.at[i, q])

                for j in range(R):
                    bacc[j] += dot(mt[i].reshape(F, T), tiles[inv[i * R + j]])

            return 0

        lax.fori_loop(0, 2, half, 0)

    def bwd_loop(n, _):
        bwd_step(n)

        @pl.when(n == Z - 1)
        def _():
            sel = wterm[pl.ds(pl.multiple_of(c * H, H), H), :].astype(F32)
            for o in range(1, C):
                arrived(wr1.at[o], w1r.at[o])
                sel += wr1[o].astype(F32)
            wr2[r] = sel.astype(BF16)
            for o in range(1, R):
                remote(wr2.at[r], wr2.at[r], w2s.at[o], w2r.at[r], (r + o) % R, c).start()

        return 0

    lax.fori_loop(0, Z + 1, bwd_loop, 0)

    def bx(o):
        to = (yo + o) % Ro
        return remote(bsend.at[o], brecv.at[o], bs.at[o], br.at[o], r - r % 2 + 1 - k, c)

    for o in list(range(1, Ro)) + [0]:
        to = (yo + o) % Ro
        bsend[o] = bacc[to * 2 + 1 - k].astype(BF16)
        bx(o).start()
    bcopies = []
    for o in range(1, Ro):
        to = (yo + o) % Ro
        arrived(brecv.at[o], br.at[o])
        osend[o] = (bacc[to * 2 + k] + brecv[o].astype(F32)).astype(BF16)
        cp = remote(osend.at[o], orecv.at[o], os_.at[o], or_.at[o], to * 2 + k, c)
        cp.start()
        bcopies.append(cp)

    for o in range(1, R):
        arrived(wr2.at[(r + o) % R], w2r.at[(r + o) % R])
    sel = wr2[0].astype(F32)
    for j in range(1, R):
        sel += wr2[j].astype(F32)
    wr3[pl.ds(pl.multiple_of(c * H, H), H), :] = (sel * scale).astype(BF16)
    mine = wr3.at[pl.ds(pl.multiple_of(c * H, H), H)]
    w3copies = []
    for o in range(1, C):
        cp = remote(mine, mine, w3s.at[o], w3r.at[c], r, (c + o) % C)
        cp.start()
        w3copies.append(cp)

    arrived(brecv.at[0], br.at[0])
    xg = bacc[r] + brecv[0].astype(F32)
    for o in range(1, Ro):
        arrived(orecv.at[o], or_.at[o])
        xg += orecv[o].astype(F32)
    xgv[...] = jnp.transpose(xg).astype(BF16)
    c_xg = pltpu.make_async_copy(xgv, xg_out, loc.at[5])
    c_xg.start()

    for o in range(1, C):
        src = (c + o) % C
        arrived(wr3.at[pl.ds(pl.multiple_of(src * H, H), H)], w3r.at[src])
    wgv[...] = wr3[...].astype(F32)
    c_wg = pltpu.make_async_copy(wgv, wg_out, loc.at[6])
    c_wg.start()

    for cp in fcopies:
        cp.wait_send()

    def sent(n, _):
        d = pick(n)
        for q in range(Q):
            px(n, q).wait_send()

            @pl.when(d != z)
            def _():
                pz(n, d, q).wait_send()

            spread(n, pick(Z - 1 - n), q, lambda cp: cp.wait_send())

        return 0

    lax.fori_loop(0, Z, sent, 0)
    for cp in w1copies + w3copies + bcopies:
        cp.wait_send()
    for o in range(1, R):
        remote(wr2.at[r], wr2.at[r], w2s.at[o], w2r.at[r], (r + o) % R, c).wait_send()
    for o in range(Ro):
        bx(o).wait_send()
    c_act.wait()
    c_xg.wait()
    c_wg.wait()


def hand_out(*refs):
    sems = refs[-1]
    copies = [pltpu.make_async_copy(refs[n], refs[3 + n], sems.at[n]) for n in range(3)]
    for cp in copies:
        cp.start()
    for cp in copies:
        cp.wait()


def local(features, adj_tiles, tile_rows, tile_cols, tile_count, weight, grad_out):
    R, C = lax.axis_size("row"), lax.axis_size("col")
    S, T = adj_tiles.shape[2], adj_tiles.shape[3]
    B, F = features.shape
    assert B == T and R % 2 == 0 and C % 2 == 0 and T % (16 * C) == 0
    Ro, Z = R // 2, C // 2
    H = T // C
    hbm = pl.BlockSpec(memory_space=pltpu.HBM)
    any_space = pl.BlockSpec(memory_space=pl.ANY)
    V = pltpu.VMEM
    dma = pltpu.SemaphoreType.DMA
    outs = pl.pallas_call(
        functools.partial(kernel, R, C, S, T, F, 1.0 / math.sqrt(B * R * C)),
        out_shape=(
            jax.ShapeDtypeStruct((B, F), BF16),
            jax.ShapeDtypeStruct((F, F), F32),
            jax.ShapeDtypeStruct((B, F), BF16),
        ),
        in_specs=[hbm] * 7,
        out_specs=(any_space, any_space, any_space),
        scratch_shapes=[
            V((S + 1, T, T), BF16), V((R, T, F), BF16), V((F, F), BF16), V((T, F), BF16),
            pltpu.SMEM((1, 1, S), jnp.int32), pltpu.SMEM((1, 1, S), jnp.int32),
            pltpu.SMEM((1, 1), jnp.int32),
            pltpu.SMEM((S,), jnp.int32), pltpu.SMEM((C * R,), jnp.int32), V((Q, T // Q, F), F32),
            V((Z, Q, T // Q, F), BF16), V((Z, Q, T // Q, F), BF16), V((Z, Q, T // Q, F), BF16),
            V((2, Z, Q, T // Q, F), BF16),
            V((T, F), BF16), V((C, Q, F // Q, T), BF16), V((R, F, T), F32),
            V((Ro, F, T), BF16), V((Ro, F, T), BF16), V((Ro, F, T), BF16), V((Ro, F, T), BF16),
            V((T, F), BF16),
            V((F, F), BF16), V((C, H, F), BF16), V((R, H, F), BF16), V((F, F), BF16),
            V((F, F), F32),
            dma((10,)), dma((2 * Ro,)), dma((R,)), dma((Z, Q)), dma((Z, Q)), dma((Z, Q)),
            dma((2, Z, Q)), dma((3, Z, Q)), dma((C, Q)), dma((Ro,)), dma((Ro,)), dma((Ro,)), dma((Ro,)),
            dma((C,)), dma((C,)), dma((R,)), dma((R,)), dma((C,)), dma((C,)),
        ],
        compiler_params=pltpu.CompilerParams(
            collective_id=0, has_side_effects=True, vmem_limit_bytes=62 * 1024 * 1024,
        ),
        cost_estimate=pl.CostEstimate(
            flops=4 * C * R * T * T * F, bytes_accessed=2 * S * T * T, transcendentals=T * F),
    )(features, adj_tiles, tile_rows, tile_cols, tile_count, weight, grad_out)
    return pl.pallas_call(
        hand_out,
        out_shape=tuple(jax.ShapeDtypeStruct(o.shape, o.dtype) for o in outs),
        in_specs=[any_space] * 3,
        out_specs=(hbm,) * 3,
        scratch_shapes=[dma((3,))],
        compiler_params=pltpu.CompilerParams(vmem_limit_bytes=62 * 1024 * 1024),
    )(*outs)


def solution(mesh):
    return jax.shard_map(
        local,
        mesh=mesh,
        in_specs=(
            P(("col", "row"), None),
            P("row", "col", None, None, None),
            P("row", "col", None),
            P("row", "col", None),
            P("row", "col"),
            P(),
            P(("row", "col"), None),
        ),
        out_specs=(P(("row", "col"), None), P(), P(("col", "row"), None)),
        check_vma=False,
    )
```

profile of v0, /device:TPU:0, one launch (start us, length us, event | category | flops | bytes accessed | tf_op | source)
XLA Modules:
  0.0 70.4 jit_solution(3668488649402823629)
XLA Ops:
  1.3 52.1 %shard_map.94 = (bf16[256,256]{1,0:T(8,128)(2,1)}, f32[256,256]{1,0:T(8,128)}, bf16[256,256]{1,0:T(8,128)(2,1)}) custom-call(bf16[256,256]{1,0:T(8,128)(2,1)} %feat.1, bf16[1,1,16,256,256]{4,3,2,1,0:T(8,128)(2,1)} %adj.1, s32[1,1,16]{2,1,0:T(1,128)} %trow.1, s32[1,1,16]{2,1,0:T(1,128)} %tcol.1, s32[1,1]{1,0:T(1,128)S(6)} %copy.10.tcnt, bf16[256,256]{1,0:T(8,128)(2,1)} %wt.1, ...), custom_call_target="tpu_custom_call" | custom-call | flops 2147483648 | bytes 2097152 | tf_op jit(solution)/shard_map/pallas_call | solution.py:375
  53.3 17.0 %shard_map.95 = (bf16[256,256]{1,0:T(8,128)(2,1)}, f32[256,256]{1,0:T(8,128)}, bf16[256,256]{1,0:T(8,128)(2,1)}) custom-call(bf16[256,256]{1,0:T(8,128)(2,1)} %get-tuple-element.6.refs_0_, f32[256,256]{1,0:T(8,128)} %get-tuple-element.7.refs_1_, bf16[256,256]{1,0:T(8,128)(2,1)} %get-tuple-element.8.refs_2_), custom_call_target="tpu_custom_call" | custom-call | tf_op jit(solution)/shard_map/pallas_call | solution.py:406
where the time goes:
time: 70.5 us; the launch traced here: 70.4 us
  Pallas kernels  69.1 us (98%)
  between operations  1.29 us (2%)
    pallas_call x1, Pallas kernels, local(): pl.pallas_call(functools.partial(kernel, R, C, S, T, F, 1.0 / math.sqrt(B...  52.1 us
    pallas_call x1, Pallas kernels, local(): pl.pallas_call(hand_out, out_shape=tuple((jax.ShapeDtypeStruct(o.shape, o...  17 us

commit v1 on v0

--- a/solution.py
+++ b/solution.py
@@ -23,7 +23,7 @@
     feat, adj, trow, tcol, tcnt, wt, gout,
     act_out, wg_out, xg_out,
     tiles, xs, wv, gv, rows_s, cols_s, cnt_s, pos, inv, accf,
-    xsend, xrecv, zsend, zrecv, actv, mt, bacc,
+    xsend, xrecv, zsend, zrecv, actv, aggv, gradv, mt, bacc,
     bsend, brecv, osend, orecv, xgv,
     wterm, wr1, wr2, wr3, wgv,
     loc, fs, fr, ps, pr, zs, zr, ms, mr, bs, br, os_, or_,
@@ -129,18 +129,20 @@
         return v
 
     def partial(i):
-        total = dot(tiles[inv[i * R]], xs[0])
-        for j in range(1, R):
-            total += dot(tiles[inv[i * R + j]], xs[j])
-        return total
+        row = jnp.concatenate([tiles[inv[i * R + j]] for j in range(R)], axis=1)
+        return dot(row, xs[...].reshape(R * T, F))
 
     def px(n, q):
         return remote(xsend.at[n, q], xrecv.at[n, q], ps.at[n, q], pr.at[n, q], r, xpeer)
 
     def fwd_peer(n, _):
         xsend[n] = partial(pick(n) * 2 + 1 - x).astype(BF16).reshape(Q, T // Q, F)
-        for q in range(Q):
-            px(n, q).start()
+
+        @pl.when(n == 0)
+        def _():
+            for q in range(Q):
+                px(0, q).start()
+
         return 0
 
     lax.fori_loop(0, Z, fwd_peer, 0)
@@ -157,6 +159,12 @@
         accf[...] = partial(d * 2 + x).reshape(Q, T // Q, F)
 
         def piece(q, _):
+            px(n, q).wait_send()
+
+            @pl.when(n < Z - 1)
+            def _():
+                px(n + 1, q).start()
+
             arrived(xrecv.at[n, q], pr.at[n, q])
             accf[q] += xrecv[n, q].astype(F32)
 
@@ -215,56 +223,47 @@
     for q in range(Q):
         spread(0, z, q, lambda cp: cp.start())
 
+    aggv[...] = agg
+    gradv[...] = grad
     actv[...] = (pre * sig).astype(BF16)
     c_act = pltpu.make_async_copy(actv, act_out, loc.at[4])
     c_act.start()
 
-    aggt = jnp.transpose(agg.astype(F32)).astype(BF16)
-    wterm[...] = dot(aggt, grad).astype(BF16)
-    w1copies = []
-    for o in range(1, C):
+    def to_row(o):
         to = (c + o) % C
-        cp = remote(wterm.at[pl.ds(pl.multiple_of(to * H, H), H)], wr1.at[o], w1s.at[o],
-                    w1r.at[o], r, to)
-        cp.start()
-        w1copies.append(cp)
-
-    for j in range(R):
-        bacc[j] = jnp.zeros((F, T), F32)
-
-    def bwd_step(n):
-        @pl.when((n > 0) & (n < Z))
+        return remote(wterm.at[pl.ds(pl.multiple_of(to * H, H), H)], wr1.at[o], w1s.at[o],
+                      w1r.at[o], r, to)
+
+    def add_blocks(blocks, first):
+        left = jnp.concatenate([mt[i].reshape(F, T) for i in blocks], axis=1)
+        for j in range(R):
+            right = jnp.concatenate([tiles[inv[i * R + j]] for i in blocks], axis=0)
+            if first:
+                bacc[j] = dot(left, right)
+            else:
+                bacc[j] += dot(left, right)
+
+    add_blocks([c], True)
+
+    def bwd_step(m, _):
+        s = pick(Z - 1 - m)
+        zi = s * 2 + x
+        for q in range(Q):
+            arrived(mt.at[zi, q], mr.at[zi, q])
+            spread(m, s, q, lambda cp: cp.start())
+        xi = pick(Z - m) * 2 + 1 - x
+        for q in range(Q):
+            arrived(mt.at[xi, q], mr.at[xi, q])
+        add_blocks([zi, xi], False)
+
+        @pl.when(m == 1)
         def _():
-            s = pick(Z - 1 - n)
-            i = s * 2 + x
-            for q in range(Q):
-                arrived(mt.at[i, q], mr.at[i, q])
-                spread(n, s, q, lambda cp: cp.start())
-
-        def half(h, _):
-            m = n - h
-
-            @pl.when((m >= 0) & (m < Z))
-            def _():
-                s = pick(Z - 1 - m)
-                i = s * 2 + jnp.where(h == 0, x, 1 - x)
-
-                @pl.when(h == 1)
-                def _():
-                    for q in range(Q):
-                        arrived(mt.at[i, q], mr.at[i, q])
-
-                for j in range(R):
-                    bacc[j] += dot(mt[i].reshape(F, T), tiles[inv[i * R + j]])
-
-            return 0
-
-        lax.fori_loop(0, 2, half, 0)
-
-    def bwd_loop(n, _):
-        bwd_step(n)
-
-        @pl.when(n == Z - 1)
+            aggt = jnp.transpose(aggv[...].astype(F32)).astype(BF16)
+            wterm[...] = dot(aggt, gradv[...]).astype(BF16)
+            for o in range(1, C):
+                to_row(o).start()
+
+        @pl.when(m == Z - 1)
         def _():
             sel = wterm[pl.ds(pl.multiple_of(c * H, H), H), :].astype(F32)
             for o in range(1, C):
@@ -276,7 +275,11 @@
 
         return 0
 
-    lax.fori_loop(0, Z + 1, bwd_loop, 0)
+    lax.fori_loop(1, Z, bwd_step, 0)
+    xi = pick(0) * 2 + 1 - x
+    for q in range(Q):
+        arrived(mt.at[xi, q], mr.at[xi, q])
+    add_blocks([xi], False)
 
     def bx(o):
         to = (yo + o) % Ro
@@ -330,8 +333,6 @@
     def sent(n, _):
         d = pick(n)
         for q in range(Q):
-            px(n, q).wait_send()
-
             @pl.when(d != z)
             def _():
                 pz(n, d, q).wait_send()
@@ -341,7 +342,9 @@
         return 0
 
     lax.fori_loop(0, Z, sent, 0)
-    for cp in w1copies + w3copies + bcopies:
+    for o in range(1, C):
+        to_row(o).wait_send()
+    for cp in w3copies + bcopies:
         cp.wait_send()
     for o in range(1, R):
         remote(wr2.at[r], wr2.at[r], w2s.at[o], w2r.at[r], (r + o) % R, c).wait_send()
@@ -353,11 +356,15 @@
 
 
 def hand_out(*refs):
-    sems = refs[-1]
-    copies = [pltpu.make_async_copy(refs[n], refs[3 + n], sems.at[n]) for n in range(3)]
-    for cp in copies:
-        cp.start()
-    for cp in copies:
+    held, sems = refs[6:9], refs[9]
+    come = [pltpu.make_async_copy(refs[n], held[n], sems.at[n]) for n in range(3)]
+    go = [pltpu.make_async_copy(held[n], refs[3 + n], sems.at[3 + n]) for n in range(3)]
+    for cp in come:
+        cp.start()
+    for n in range(3):
+        come[n].wait()
+        go[n].start()
+    for cp in go:
         cp.wait()
 
 
@@ -388,7 +395,7 @@
             pltpu.SMEM((S,), jnp.int32), pltpu.SMEM((C * R,), jnp.int32), V((Q, T // Q, F), F32),
             V((Z, Q, T // Q, F), BF16), V((Z, Q, T // Q, F), BF16), V((Z, Q, T // Q, F), BF16),
             V((2, Z, Q, T // Q, F), BF16),
-            V((T, F), BF16), V((C, Q, F // Q, T), BF16), V((R, F, T), F32),
+            V((T, F), BF16), V((T, F), BF16), V((T, F), BF16), V((C, Q, F // Q, T), BF16), V((R, F, T), F32),
             V((Ro, F, T), BF16), V((Ro, F, T), BF16), V((Ro, F, T), BF16), V((Ro, F, T), BF16),
             V((T, F), BF16),
             V((F, F), BF16), V((C, H, F), BF16), V((R, H, F), BF16), V((F, F), BF16),
@@ -408,7 +415,7 @@
         out_shape=tuple(jax.ShapeDtypeStruct(o.shape, o.dtype) for o in outs),
         in_specs=[any_space] * 3,
         out_specs=(hbm,) * 3,
-        scratch_shapes=[dma((3,))],
+        scratch_shapes=[V(o.shape, o.dtype) for o in outs] + [dma((6,))],
         compiler_params=pltpu.CompilerParams(vmem_limit_bytes=62 * 1024 * 1024),
     )(*outs)
 

time: 70.5 us -> 56.7 us (0.80)
  Pallas kernels: 69.1 us -> 55.3 us
    pallas_call x1, Pallas kernels: 17 us -> 1.81 us  [local(): pl.pallas_call(hand_out, out_shape=tuple((jax.ShapeDtypeStruct(o.shape, o...]
    pallas_call x1, Pallas kernels: 52.1 us -> 53.4 us  [local(): pl.pallas_call(functools.partial(kernel, R, C, S, T, F, 1.0 / math.sqrt(B...]
where the time goes in v1:
time: 56.7 us; the launch traced here: 56.5 us
  Pallas kernels  55.3 us (98%)
  between operations  1.29 us (2%)
    pallas_call x1, Pallas kernels, local(): pl.pallas_call(functools.partial(kernel, R, C, S, T, F, 1.0 / math.sqrt(B...  53.4 us
    pallas_call x1, Pallas kernels, local(): pl.pallas_call(hand_out, out_shape=tuple((jax.ShapeDtypeStruct(o.shape, o...  1.81 us

profile of v1, /device:TPU:0, one launch (start us, length us, event | category | flops | bytes accessed | tf_op | source)
XLA Modules:
  0.0 56.5 jit_solution(3558613569669493937)
XLA Ops:
  1.3 53.4 %shard_map.94 = (bf16[256,256]{1,0:T(8,128)(2,1)}, f32[256,256]{1,0:T(8,128)}, bf16[256,256]{1,0:T(8,128)(2,1)}) custom-call(bf16[256,256]{1,0:T(8,128)(2,1)} %feat.1, bf16[1,1,16,256,256]{4,3,2,1,0:T(8,128)(2,1)} %adj.1, s32[1,1,16]{2,1,0:T(1,128)} %trow.1, s32[1,1,16]{2,1,0:T(1,128)} %tcol.1, s32[1,1]{1,0:T(1,128)S(6)} %copy.10.tcnt, bf16[256,256]{1,0:T(8,128)(2,1)} %wt.1, ...), custom_call_target="tpu_custom_call" | custom-call | flops 2147483648 | bytes 2097152 | tf_op jit(solution)/shard_map/pallas_call | solution.py:382
  54.7 1.8 %shard_map.95 = (bf16[256,256]{1,0:T(8,128)(2,1)}, f32[256,256]{1,0:T(8,128)}, bf16[256,256]{1,0:T(8,128)(2,1)}) custom-call(bf16[256,256]{1,0:T(8,128)(2,1)} %get-tuple-element.6.refs_0_, f32[256,256]{1,0:T(8,128)} %get-tuple-element.7.refs_1_, bf16[256,256]{1,0:T(8,128)(2,1)} %get-tuple-element.8.refs_2_), custom_call_target="tpu_custom_call" | custom-call | tf_op jit(solution)/shard_map/pallas_call | solution.py:413

commit v2 on v1

--- a/solution.py
+++ b/solution.py
@@ -11,7 +11,7 @@
 MESH = pl.DeviceIdType.MESH
 BF16 = jnp.bfloat16
 F32 = jnp.float32
-Q = 2
+Q = 4
 
 
 def dot(a, b):

time: 56.7 us -> 56.8 us (level)
  no operation moved by 1% of the time
where the time goes in v2:
time: 56.8 us; the launch traced here: 56.6 us
  Pallas kernels  55.3 us (97%)
  between operations  1.29 us (2%)
    pallas_call x1, Pallas kernels, local(): pl.pallas_call(functools.partial(kernel, R, C, S, T, F, 1.0 / math.sqrt(B...  53.5 us
    pallas_call x1, Pallas kernels, local(): pl.pallas_call(hand_out, out_shape=tuple((jax.ShapeDtypeStruct(o.shape, o...  1.81 us

profile of v2, /device:TPU:0, one launch (start us, length us, event | category | flops | bytes accessed | tf_op | source)
XLA Modules:
  0.0 56.6 jit_solution(17199127223237583936)
XLA Ops:
  1.3 53.5 %shard_map.94 = (bf16[256,256]{1,0:T(8,128)(2,1)}, f32[256,256]{1,0:T(8,128)}, bf16[256,256]{1,0:T(8,128)(2,1)}) custom-call(bf16[256,256]{1,0:T(8,128)(2,1)} %feat.1, bf16[1,1,16,256,256]{4,3,2,1,0:T(8,128)(2,1)} %adj.1, s32[1,1,16]{2,1,0:T(1,128)} %trow.1, s32[1,1,16]{2,1,0:T(1,128)} %tcol.1, s32[1,1]{1,0:T(1,128)S(6)} %copy.10.tcnt, bf16[256,256]{1,0:T(8,128)(2,1)} %wt.1, ...), custom_call_target="tpu_custom_call" | custom-call | flops 2147483648 | bytes 2097152 | tf_op jit(solution)/shard_map/pallas_call | solution.py:382
  54.8 1.8 %shard_map.95 = (bf16[256,256]{1,0:T(8,128)(2,1)}, f32[256,256]{1,0:T(8,128)}, bf16[256,256]{1,0:T(8,128)(2,1)}) custom-call(bf16[256,256]{1,0:T(8,128)(2,1)} %get-tuple-element.6.refs_0_, f32[256,256]{1,0:T(8,128)} %get-tuple-element.7.refs_1_, bf16[256,256]{1,0:T(8,128)(2,1)} %get-tuple-element.8.refs_2_), custom_call_target="tpu_custom_call" | custom-call | tf_op jit(solution)/shard_map/pallas_call | solution.py:413

commit v3 on v1

--- a/solution.py
+++ b/solution.py
@@ -23,7 +23,7 @@
     feat, adj, trow, tcol, tcnt, wt, gout,
     act_out, wg_out, xg_out,
     tiles, xs, wv, gv, rows_s, cols_s, cnt_s, pos, inv, accf,
-    xsend, xrecv, zsend, zrecv, actv, aggv, gradv, mt, bacc,
+    xsend, xrecv, xside, zsend, zrecv, actv, aggv, gradv, mt, bacc,
     bsend, brecv, osend, orecv, xgv,
     wterm, wr1, wr2, wr3, wgv,
     loc, fs, fr, ps, pr, zs, zr, ms, mr, bs, br, os_, or_,
@@ -132,6 +132,15 @@
         row = jnp.concatenate([tiles[inv[i * R + j]] for j in range(R)], axis=1)
         return dot(row, xs[...].reshape(R * T, F))
 
+    side = z + 1 - 2 * (z % 2)
+    at_side = jnp.int32(0)
+    for kk in range(Z):
+        at_side = jnp.where(order[kk] == side, jnp.int32(kk), at_side)
+    c_side = remote(xsend.at[at_side, Q - 1], xside, loc.at[10], loc.at[11], r, side * 2 + x)
+
+    def over_x(n, q):
+        return jnp.logical_not((n == at_side) & (q == Q - 1))
+
     def px(n, q):
         return remote(xsend.at[n, q], xrecv.at[n, q], ps.at[n, q], pr.at[n, q], r, xpeer)
 
@@ -146,6 +155,7 @@
         return 0
 
     lax.fori_loop(0, Z, fwd_peer, 0)
+    c_side.start()
 
     def pz(n, d, q):
         right = d > z
@@ -159,14 +169,24 @@
         accf[...] = partial(d * 2 + x).reshape(Q, T // Q, F)
 
         def piece(q, _):
-            px(n, q).wait_send()
-
-            @pl.when(n < Z - 1)
+            @pl.when(over_x(n, q))
+            def _():
+                px(n, q).wait_send()
+
+            @pl.when((n + 1 == Z - 1) & (q == Q - 1))
+            def _():
+                arrived(xside, loc.at[11])
+                xsend[Z - 1, Q - 1] = (
+                    xsend[Z - 1, Q - 1].astype(F32) + xside[...].astype(F32)).astype(BF16)
+
+            @pl.when((n < Z - 1) & over_x(n + 1, q))
             def _():
                 px(n + 1, q).start()
 
-            arrived(xrecv.at[n, q], pr.at[n, q])
-            accf[q] += xrecv[n, q].astype(F32)
+            @pl.when(over_x(n, q))
+            def _():
+                arrived(xrecv.at[n, q], pr.at[n, q])
+                accf[q] += xrecv[n, q].astype(F32)
 
             @pl.when((d >= z) & (z > 0))
             def _():
@@ -218,7 +238,9 @@
         def _():
             act(to_z(n, s, q, 1))
 
-        act(to_peer(n, s, q))
+        @pl.when((s != side) | (q != Q - 1))
+        def _():
+            act(to_peer(n, s, q))
 
     for q in range(Q):
         spread(0, z, q, lambda cp: cp.start())
@@ -243,6 +265,8 @@
             else:
                 bacc[j] += dot(left, right)
 
+    c_back = remote(mt.at[xpeer, Q - 1], mt.at[xpeer, Q - 1], loc.at[12], mr.at[xpeer, Q - 1], r,
+                    side * 2 + x)
     add_blocks([c], True)
 
     def bwd_step(m, _):
@@ -254,6 +278,11 @@
         xi = pick(Z - m) * 2 + 1 - x
         for q in range(Q):
             arrived(mt.at[xi, q], mr.at[xi, q])
+
+        @pl.when(m == 1)
+        def _():
+            c_back.start()
+
         add_blocks([zi, xi], False)
 
         @pl.when(m == 1)
@@ -327,6 +356,8 @@
     c_wg = pltpu.make_async_copy(wgv, wg_out, loc.at[6])
     c_wg.start()
 
+    c_side.wait_send()
+    c_back.wait_send()
     for cp in fcopies:
         cp.wait_send()
 
@@ -372,7 +403,7 @@
     R, C = lax.axis_size("row"), lax.axis_size("col")
     S, T = adj_tiles.shape[2], adj_tiles.shape[3]
     B, F = features.shape
-    assert B == T and R % 2 == 0 and C % 2 == 0 and T % (16 * C) == 0
+    assert B == T and R % 2 == 0 and C % 4 == 0 and C >= 8 and T % (16 * C) == 0
     Ro, Z = R // 2, C // 2
     H = T // C
     hbm = pl.BlockSpec(memory_space=pltpu.HBM)
@@ -393,14 +424,15 @@
             pltpu.SMEM((1, 1, S), jnp.int32), pltpu.SMEM((1, 1, S), jnp.int32),
             pltpu.SMEM((1, 1), jnp.int32),
             pltpu.SMEM((S,), jnp.int32), pltpu.SMEM((C * R,), jnp.int32), V((Q, T // Q, F), F32),
-            V((Z, Q, T // Q, F), BF16), V((Z, Q, T // Q, F), BF16), V((Z, Q, T // Q, F), BF16),
+            V((Z, Q, T // Q, F), BF16), V((Z, Q, T // Q, F), BF16), V((T // Q, F), BF16),
+            V((Z, Q, T // Q, F), BF16),
             V((2, Z, Q, T // Q, F), BF16),
             V((T, F), BF16), V((T, F), BF16), V((T, F), BF16), V((C, Q, F // Q, T), BF16), V((R, F, T), F32),
             V((Ro, F, T), BF16), V((Ro, F, T), BF16), V((Ro, F, T), BF16), V((Ro, F, T), BF16),
             V((T, F), BF16),
             V((F, F), BF16), V((C, H, F), BF16), V((R, H, F), BF16), V((F, F), BF16),
             V((F, F), F32),
-            dma((10,)), dma((2 * Ro,)), dma((R,)), dma((Z, Q)), dma((Z, Q)), dma((Z, Q)),
+            dma((13,)), dma((2 * Ro,)), dma((R,)), dma((Z, Q)), dma((Z, Q)), dma((Z, Q)),
             dma((2, Z, Q)), dma((3, Z, Q)), dma((C, Q)), dma((Ro,)), dma((Ro,)), dma((Ro,)), dma((Ro,)),
             dma((C,)), dma((C,)), dma((R,)), dma((R,)), dma((C,)), dma((C,)),
         ],

time: 56.7 us -> 57.2 us (level)
  no operation moved by 1% of the time
where the time goes in v3:
time: 57.2 us; the launch traced here: 57 us
  Pallas kernels  55.7 us (97%)
  between operations  1.29 us (2%)
    pallas_call x1, Pallas kernels, local(): pl.pallas_call(functools.partial(kernel, R, C, S, T, F, 1.0 / math.sqrt(B...  53.9 us
    pallas_call x1, Pallas kernels, local(): pl.pallas_call(hand_out, out_shape=tuple((jax.ShapeDtypeStruct(o.shape, o...  1.81 us

profile of v3, /device:TPU:0, one launch (start us, length us, event | category | flops | bytes accessed | tf_op | source)
XLA Modules:
  0.0 57.0 jit_solution(10855642667728726412)
XLA Ops:
  1.3 53.9 %shard_map.94 = (bf16[256,256]{1,0:T(8,128)(2,1)}, f32[256,256]{1,0:T(8,128)}, bf16[256,256]{1,0:T(8,128)(2,1)}) custom-call(bf16[256,256]{1,0:T(8,128)(2,1)} %feat.1, bf16[1,1,16,256,256]{4,3,2,1,0:T(8,128)(2,1)} %adj.1, s32[1,1,16]{2,1,0:T(1,128)} %trow.1, s32[1,1,16]{2,1,0:T(1,128)} %tcol.1, s32[1,1]{1,0:T(1,128)S(6)} %copy.10.tcnt, bf16[256,256]{1,0:T(8,128)(2,1)} %wt.1, ...), custom_call_target="tpu_custom_call" | custom-call | flops 2147483648 | bytes 2097152 | tf_op jit(solution)/shard_map/pallas_call | solution.py:413
  55.2 1.8 %shard_map.95 = (bf16[256,256]{1,0:T(8,128)(2,1)}, f32[256,256]{1,0:T(8,128)}, bf16[256,256]{1,0:T(8,128)(2,1)}) custom-call(bf16[256,256]{1,0:T(8,128)(2,1)} %get-tuple-element.6.refs_0_, f32[256,256]{1,0:T(8,128)} %get-tuple-element.7.refs_1_, bf16[256,256]{1,0:T(8,128)(2,1)} %get-tuple-element.8.refs_2_), custom_call_target="tpu_custom_call" | custom-call | tf_op jit(solution)/shard_map/pallas_call | solution.py:445

commit v4 on v1

--- a/solution.py
+++ b/solution.py
@@ -74,15 +74,28 @@
 
     c_feat.wait()
     fcopies = []
-    for o in range(1, Ro):
-        cp = remote(xs.at[r], xs.at[r], fs.at[o], fr.at[r], ((yo + o) % Ro) * 2 + k, c)
+
+    def send_feat(j, q, sem, row):
+        part = xs.at[j, pl.ds(q * (T // Q), T // Q)]
+        cp = remote(part, part, fs.at[sem, q], fr.at[j, q], row, c)
         cp.start()
         fcopies.append(cp)
-    cp = remote(xs.at[r], xs.at[r], fs.at[0], fr.at[r], inner, c)
-    cp.start()
-    fcopies.append(cp)
-
+
+    def wait_feat(j, q):
+        arrived(xs.at[j, pl.ds(q * (T // Q), T // Q)], fr.at[j, q])
+
+    for q in range(Q):
+        for o in range(1, Ro):
+            send_feat(r, q, o, ((yo + o) % Ro) * 2 + k)
+    for q in range(Q):
+        send_feat(r, q, 0, inner)
     tiles[S] = jnp.zeros((T, T), BF16)
+    for o in range(1, Ro):
+        j = ((yo - o + Ro) % Ro) * 2 + k
+        for q in range(Q):
+            wait_feat(j, q)
+            send_feat(j, q, Ro - 1 + o, inner)
+
     for cp in c_ids:
         cp.wait()
     total = cnt_s[0, 0]
@@ -102,17 +115,11 @@
 
     lax.fori_loop(0, C * R, set_inv, 0)
 
-    for o in range(1, Ro):
-        j = ((yo - o + Ro) % Ro) * 2 + k
-        arrived(xs.at[j], fr.at[j])
-        cp = remote(xs.at[j], xs.at[j], fs.at[Ro - 1 + o], fr.at[j], inner, c)
-        cp.start()
-        fcopies.append(cp)
-    arrived(xs.at[inner], fr.at[inner])
     c_adj.wait()
-    for o in range(1, Ro):
-        j = ((yo - o + Ro) % Ro) * 2 + 1 - k
-        arrived(xs.at[j], fr.at[j])
+    for q in range(Q):
+        wait_feat(inner, q)
+        for o in range(1, Ro):
+            wait_feat(((yo - o + Ro) % Ro) * 2 + 1 - k, q)
 
     tables = [sorted(range(Z), key=lambda d, zz=zz: (-abs(d - zz), d)) for zz in range(Z)]
     order = []
@@ -400,7 +407,7 @@
             V((T, F), BF16),
             V((F, F), BF16), V((C, H, F), BF16), V((R, H, F), BF16), V((F, F), BF16),
             V((F, F), F32),
-            dma((10,)), dma((2 * Ro,)), dma((R,)), dma((Z, Q)), dma((Z, Q)), dma((Z, Q)),
+            dma((10,)), dma((2 * Ro, Q)), dma((R, Q)), dma((Z, Q)), dma((Z, Q)), dma((Z, Q)),
             dma((2, Z, Q)), dma((3, Z, Q)), dma((C, Q)), dma((Ro,)), dma((Ro,)), dma((Ro,)), dma((Ro,)),
             dma((C,)), dma((C,)), dma((R,)), dma((R,)), dma((C,)), dma((C,)),
         ],

time: 56.7 us -> 58.1 us (1.025)
  Pallas kernels: 55.3 us -> 56.6 us
    pallas_call x1, Pallas kernels: 53.4 us -> 54.8 us  [local(): pl.pallas_call(functools.partial(kernel, R, C, S, T, F, 1.0 / math.sqrt(B...]
where the time goes in v4:
time: 58.1 us; the launch traced here: 57.9 us
  Pallas kernels  56.6 us (97%)
  between operations  1.29 us (2%)
    pallas_call x1, Pallas kernels, local(): pl.pallas_call(functools.partial(kernel, R, C, S, T, F, 1.0 / math.sqrt(B...  54.8 us
    pallas_call x1, Pallas kernels, local(): pl.pallas_call(hand_out, out_shape=tuple((jax.ShapeDtypeStruct(o.shape, o...  1.81 us

profile of v4, /device:TPU:0, one launch (start us, length us, event | category | flops | bytes accessed | tf_op | source)
XLA Modules:
  0.0 57.9 jit_solution(10779553788003153970)
XLA Ops:
  1.3 54.8 %shard_map.94 = (bf16[256,256]{1,0:T(8,128)(2,1)}, f32[256,256]{1,0:T(8,128)}, bf16[256,256]{1,0:T(8,128)(2,1)}) custom-call(bf16[256,256]{1,0:T(8,128)(2,1)} %feat.1, bf16[1,1,16,256,256]{4,3,2,1,0:T(8,128)(2,1)} %adj.1, s32[1,1,16]{2,1,0:T(1,128)} %trow.1, s32[1,1,16]{2,1,0:T(1,128)} %tcol.1, s32[1,1]{1,0:T(1,128)S(6)} %copy.10.tcnt, bf16[256,256]{1,0:T(8,128)(2,1)} %wt.1, ...), custom_call_target="tpu_custom_call" | custom-call | flops 2147483648 | bytes 2097152 | tf_op jit(solution)/shard_map/pallas_call | solution.py:389
  56.0 1.8 %shard_map.95 = (bf16[256,256]{1,0:T(8,128)(2,1)}, f32[256,256]{1,0:T(8,128)}, bf16[256,256]{1,0:T(8,128)(2,1)}) custom-call(bf16[256,256]{1,0:T(8,128)(2,1)} %get-tuple-element.6.refs_0_, f32[256,256]{1,0:T(8,128)} %get-tuple-element.7.refs_1_, bf16[256,256]{1,0:T(8,128)(2,1)} %get-tuple-element.8.refs_2_), custom_call_target="tpu_custom_call" | custom-call | tf_op jit(solution)/shard_map/pallas_call | solution.py:420

commit v5 on v1

--- a/solution.py
+++ b/solution.py
@@ -93,14 +93,16 @@
 
     lax.fori_loop(0, S, set_pos, 0)
 
-    def set_inv(p, _):
-        slot = jnp.int32(S)
+    def set_inv(step, _):
+        slots = [jnp.int32(S)] * 8
         for s in range(S):
-            slot = jnp.where(pos[s] == p, jnp.int32(s), slot)
-        inv[p] = slot
-        return 0
-
-    lax.fori_loop(0, C * R, set_inv, 0)
+            held = pos[s] - step * 8
+            slots = [jnp.where(held == u, jnp.int32(s), slots[u]) for u in range(8)]
+        for u in range(8):
+            inv[step * 8 + u] = slots[u]
+        return 0
+
+    lax.fori_loop(0, C * R // 8, set_inv, 0)
 
     for o in range(1, Ro):
         j = ((yo - o + Ro) % Ro) * 2 + k
@@ -372,7 +374,7 @@
     R, C = lax.axis_size("row"), lax.axis_size("col")
     S, T = adj_tiles.shape[2], adj_tiles.shape[3]
     B, F = features.shape
-    assert B == T and R % 2 == 0 and C % 2 == 0 and T % (16 * C) == 0
+    assert B == T and R % 2 == 0 and C % 2 == 0 and T % (16 * C) == 0 and C * R % 8 == 0
     Ro, Z = R // 2, C // 2
     H = T // C
     hbm = pl.BlockSpec(memory_space=pltpu.HBM)

time: 56.7 us -> 56.7 us (level)
  no operation moved by 1% of the time
where the time goes in v5:
time: 56.7 us; the launch traced here: 56.5 us
  Pallas kernels  55.3 us (98%)
  between operations  1.29 us (2%)
    pallas_call x1, Pallas kernels, local(): pl.pallas_call(functools.partial(kernel, R, C, S, T, F, 1.0 / math.sqrt(B...  53.4 us
    pallas_call x1, Pallas kernels, local(): pl.pallas_call(hand_out, out_shape=tuple((jax.ShapeDtypeStruct(o.shape, o...  1.81 us

profile of v5, /device:TPU:0, one launch (start us, length us, event | category | flops | bytes accessed | tf_op | source)
XLA Modules:
  0.0 56.5 jit_solution(5892237269408335151)
XLA Ops:
  1.3 53.4 %shard_map.94 = (bf16[256,256]{1,0:T(8,128)(2,1)}, f32[256,256]{1,0:T(8,128)}, bf16[256,256]{1,0:T(8,128)(2,1)}) custom-call(bf16[256,256]{1,0:T(8,128)(2,1)} %feat.1, bf16[1,1,16,256,256]{4,3,2,1,0:T(8,128)(2,1)} %adj.1, s32[1,1,16]{2,1,0:T(1,128)} %trow.1, s32[1,1,16]{2,1,0:T(1,128)} %tcol.1, s32[1,1]{1,0:T(1,128)S(6)} %copy.10.tcnt, bf16[256,256]{1,0:T(8,128)(2,1)} %wt.1, ...), custom_call_target="tpu_custom_call" | custom-call | flops 2147483648 | bytes 2097152 | tf_op jit(solution)/shard_map/pallas_call | solution.py:384
  54.7 1.8 %shard_map.95 = (bf16[256,256]{1,0:T(8,128)(2,1)}, f32[256,256]{1,0:T(8,128)}, bf16[256,256]{1,0:T(8,128)(2,1)}) custom-call(bf16[256,256]{1,0:T(8,128)(2,1)} %get-tuple-element.6.refs_0_, f32[256,256]{1,0:T(8,128)} %get-tuple-element.7.refs_1_, bf16[256,256]{1,0:T(8,128)(2,1)} %get-tuple-element.8.refs_2_), custom_call_target="tpu_custom_call" | custom-call | tf_op jit(solution)/shard_map/pallas_call | solution.py:415
